TPU v7x, 256 devices: a whole 4x4x8 slice. The times are simulated.
256 devices in a mesh: doc: 32 (over x, z), cent: 8 (over y, core).
Axes of the slice: x: 4, y: 4, z: 8, core: 2. Of those that a mesh axis runs over, the one named last changes fastest.
Arguments:
- embeddings: float32 [65536, 1024], P('doc', 'cent'), may hold values from -320 to 320
- row_mask: int32 [65536], P('doc'), may hold values from 0 to 1, as said below
- block_cluster: int32 [512], P('doc'), may hold values from 0 to 100351, as said below
- candidates: int32 [65536, 8], P('doc'), may hold values from 0 to 100351, as said below
- old_centroids: float32 [100352, 1024], P('doc', 'cent'), may hold values from -0.1875 to 0.1875
Outputs:
- member_sums: float32 [100352, 1024], P('doc', 'cent')
- member_counts: int32 [100352], P('doc')
- centroids: float32 [100352, 1024], P('doc', 'cent')
- cosines: float32 [65536, 8], P(('doc', 'cent'))
Inputs may be any that keep to these rules, and one draw needn't show every extreme that they name: `row_mask`: in each block of 128 rows the live rows come first, at least one; the first block of each 2048 rows is full. `block_cluster`: within the blocks of one index of doc the values never fall. Those blocks name centroids of the range c * 3136 to c * 3136 + 3135 in at most 2 blocks, for every c; in every draw some range is named in exactly 2 blocks of every index of doc. `candidates`: of the 16384 ids of the rows of one index of doc, exactly 512 lie in each range c * 3136 to c * 3136 + 3135.
All inputs are finite; a program needn't handle non-finite values.
Results may differ from a plain program's by a relative error of at most 0.0003.
Values sent between devices are 32-bit elements; how exact they have to be, the bound alone decides.
A program may use at most 128 MiB of HBM per device.

v0:
```python
import jax
import jax.numpy as jnp
from jax import lax
from jax.sharding import PartitionSpec as P


def on_device(embeddings, row_mask, block_cluster, candidates, old_centroids):
    row_count, feat_width = embeddings.shape
    owners = lax.axis_size("doc")
    pieces = lax.axis_size("cent")
    per_owner = old_centroids.shape[0]
    live_rows = row_mask.astype(jnp.float32)
    squares = lax.psum(jnp.sum(embeddings * embeddings, axis=1), "cent")
    unit_rows = embeddings * lax.rsqrt(squares + 1e-06)[:, None]
    highest = lax.Precision.HIGHEST
    block_count = block_cluster.shape[0]
    block_rows = row_count // block_count
    block_sums = jnp.sum(
        (unit_rows * live_rows[:, None]).reshape(block_count, block_rows, feat_width), axis=1
    )
    block_counts = jnp.sum(live_rows.reshape(block_count, block_rows), axis=1)
    capacity = max(2, 2 * block_count // owners)
    block_owner = block_cluster // per_owner
    local_id = block_cluster - block_owner * per_owner
    earlier = jnp.arange(block_count)[None, :] < jnp.arange(block_count)[:, None]
    same_owner = block_owner[None, :] == block_owner[:, None]
    block_rank = jnp.sum(jnp.logical_and(earlier, same_owner), axis=1)
    slot_index = block_owner * capacity + block_rank
    placing = (jnp.arange(owners * capacity)[:, None] == slot_index[None, :]).astype(jnp.float32)
    slot_sums = jnp.dot(placing, block_sums, precision=highest).reshape(
        owners, capacity, feat_width
    )
    slot_ids = jnp.dot(placing, local_id.astype(jnp.float32), precision=highest).reshape(
        owners, capacity
    )
    slot_counts = jnp.dot(placing, block_counts, precision=highest).reshape(owners, capacity)
    recv_sums, recv_ids, recv_counts = (
        lax.all_to_all(slot_sums, "doc", split_axis=0, concat_axis=0, tiled=True),
        lax.all_to_all(slot_ids, "doc", split_axis=0, concat_axis=0, tiled=True),
        lax.all_to_all(slot_counts, "doc", split_axis=0, concat_axis=0, tiled=True),
    )
    taking = (
        jnp.arange(per_owner)[:, None] == recv_ids.reshape(-1).astype(jnp.int32)[None, :]
    ).astype(jnp.float32)
    member_sums = jnp.dot(taking, recv_sums.reshape(-1, feat_width), precision=highest)
    counts = jnp.dot(taking, recv_counts.reshape(-1), precision=highest)
    cent_squares = lax.psum(jnp.sum(member_sums * member_sums, axis=1), "cent")
    centroids = jnp.where(
        counts[:, None] > 0, member_sums * lax.rsqrt(cent_squares + 1e-06)[:, None], old_centroids
    )
    cand_count = candidates.shape[1]
    flat_ids = candidates.reshape(-1)
    total_ids = flat_ids.shape[0]
    cand_owner = flat_ids // per_owner
    tile_width = 128
    tile_count = total_ids // tile_width
    owner_table = (
        (cand_owner[:, None] == jnp.arange(owners)[None, :])
        .astype(jnp.float32)
        .reshape(tile_count, tile_width, owners)
    )
    lower = (jnp.arange(tile_width)[:, None] > jnp.arange(tile_width)[None, :]).astype(jnp.float32)
    within = jnp.einsum("ij,bjo->bio", lower, owner_table, precision=highest)
    tile_totals = jnp.sum(owner_table, axis=1)
    offsets = jnp.cumsum(tile_totals, axis=0) - tile_totals
    id_rank = (
        jnp.sum((within + offsets[:, None, :]) * owner_table, axis=-1)
        .reshape(total_ids)
        .astype(jnp.int32)
    )
    per_peer = total_ids // owners
    position = cand_owner * per_peer + id_rank
    ordering = (
        jnp.zeros((total_ids,), jnp.int32).at[position].set(jnp.arange(total_ids, dtype=jnp.int32))
    )
    sorted_ids = (flat_ids - cand_owner * per_owner)[ordering].reshape(owners, per_peer)
    source_row = ordering // cand_count
    own_rows = unit_rows[source_row].reshape(owners, per_peer, feat_width)
    picked = centroids[lax.all_to_all(sorted_ids, "doc", split_axis=0, concat_axis=0, tiled=True)]
    vectors = lax.all_to_all(picked, "doc", split_axis=0, concat_axis=0, tiled=True)
    sorted_dots = jnp.sum(vectors * own_rows, axis=-1).reshape(-1)
    products = sorted_dots[position].reshape(row_count, cand_count)
    shared = lax.psum_scatter(products, "cent", scatter_dimension=0, tiled=True)
    share_rows = row_count // pieces
    my_live = lax.dynamic_slice_in_dim(live_rows, lax.axis_index("cent") * share_rows, share_rows)
    return (member_sums, counts.astype(jnp.int32), centroids, shared * my_live[:, None])


def solution(mesh):
    placed = (P("doc", "cent"), P("doc"), P("doc"), P("doc", None), P("doc", "cent"))
    return jax.shard_map(
        on_device,
        mesh=mesh,
        in_specs=placed,
        out_specs=(P("doc", "cent"), P("doc"), P("doc", "cent"), P(("doc", "cent"), None)),
        check_vma=False,
    )
```

profile of v0, /device:TPU:1, one launch (start us, length us, event | category | flops | bytes accessed | tf_op | source)
XLA Modules:
  0.0 734.0 jit_solution(3682147388347804066)
XLA Ops:
  7.2 0.7 and_select_fusion
  7.8 0.2 convert_reduce_fusion.2
  8.0 0.7 multiply_add_fusion.1
  8.7 0.8 bitcast_reduce_fusion.1
  9.5 0.2 fusion.25
  9.7 0.7 copy.34
  10.4 11.9 %all-to-all-start.2 = ((f32[32,1,2]{2,1,0:T(1,128)}), f32[32,1,2]{2,1,0:T(1,128)S(1)}, u32[]{:S(2)}, u32[]{:S(2)}) async-start(f32[32,1,2]{2,1,0:T(1,128)} %copy.34), calls=%async_computation.2 | async-start | bytes 32768 | tf_op jit(solution)/shard_map/all_to_all | solution.py:40
  22.3 0.9 fusion.16
  23.2 0.9 broadcast_divide_fusion
  24.0 0.4 copy.36
  24.5 0.5 and.39
  25.0 0.5 and.38
  25.5 0.3 copy.37
  25.9 0.5 div.44
  26.4 0.5 div.43
  26.9 0.3 copy.35
  27.3 0.3 multiply_reduce_fusion.2
  27.6 13.1 %psum.14 = f32[2048]{0:T(1024)S(1)} all-reduce(f32[2048]{0:T(1024)S(1)} %multiply_reduce_fusion.2), channel_id=1, replica_groups=mesh['doc'=32,'cent'=8] {'cent'}, use_global_device_ids=true, to_apply=%region_2.0 | all-reduce | flops 2048 | bytes 16384 | tf_op jit(solution)/shard_map/psum | solution.py:13
  40.8 0.4 convert_reduce_fusion
  41.5 0.8 fusion
  42.5 60.3 %scatter_custom_fusion = s32[16384]{0:T(1024)S(1)} fusion(s32[16384]{0:T(1024)S(1)} %bitcast.46, s32[16384]{0:T(1024)S(1)} %iota.50, s32[]{:T(128)} %constant.25.clone.1), kind=kCustom, calls=%fused_computation.57 | custom fusion | bytes 65540 | tf_op jit(solution)/shard_map/scatter | solution.py:74
  102.9 0.5 reshape.239
  103.6 0.8 all_to_all.26
  104.4 0.6 bitcast_reduce_fusion
  105.0 9.5 %all-to-all-start = ((f32[32,1,2]{2,1,0:T(1,128)}), f32[32,1,2]{2,1,0:T(1,128)S(1)}, u32[]{:S(2)}, u32[]{:S(2)}) async-start(f32[32,1,2]{2,1,0:T(1,128)} %bitcast.2), calls=%async_computation | async-start | bytes 32768 | tf_op jit(solution)/shard_map/all_to_all | solution.py:39
  114.5 0.3 fusion.22
  114.8 0.6 copy.33
  115.5 160.3 %gather_fusion = s32[16384]{0:T(1024)} fusion(s32[16384]{0:T(1024)S(1)} %fusion.9, s32[16384]{0:T(1024)S(1)} %get-tuple-element.19), kind=kCustom, calls=%fused_computation | custom fusion | bytes 196608 | tf_op jit(solution)/shard_map/gather | solution.py:76
  275.7 0.5 broadcast.193
  276.2 0.7 reduce.9
  277.0 9.2 %all-to-all-start.1 = ((f32[32,2,128]{2,1,0:T(2,128)}), f32[32,2,128]{2,1,0:T(2,128)S(1)}, u32[]{:S(2)}, u32[]{:S(2)}) async-start(f32[32,2,128]{2,1,0:T(2,128)} %copy.33), calls=%async_computation.1 | async-start | bytes 65536 | tf_op jit(solution)/shard_map/all_to_all | solution.py:38
  286.5 0.9 fusion.4
  287.4 7.7 %all-to-all-done.1 = f32[32,2,128]{2,1,0:T(2,128)S(1)} async-done(((f32[32,2,128]{2,1,0:T(2,128)}), f32[32,2,128]{2,1,0:T(2,128)S(1)}, u32[]{:S(2)}, u32[]{:S(2)}) %all-to-all-start.1) | async-done | bytes 32800 | tf_op jit(solution)/shard_map/all_to_all | solution.py:38
  295.1 3.9 all-to-all-start.3
  298.9 2.0 multiply_reduce_fusion.1
  300.9 24.9 %psum.15 = f32[3136]{0:T(1024)S(1)} all-reduce(f32[3136]{0:T(1024)S(1)} %get-tuple-element.20), channel_id=1, replica_groups=mesh['doc'=32,'cent'=8] {'cent'}, use_global_device_ids=true, to_apply=%region_6.7 | all-reduce | flops 3136 | bytes 25088 | tf_op jit(solution)/shard_map/psum | solution.py:47
  325.8 3.8 multiply_select_fusion
  329.7 54.4 %gather_fusion.1 = f32[16384,128]{1,0:T(8,128)} fusion(f32[3136,128]{1,0:T(8,128)S(1)} %multiply_select_fusion, s32[16384]{0:T(1024)S(1)} %broadcast_clamp_fusion), kind=kCustom, calls=%fused_computation.1 | custom fusion | bytes 16842752 | tf_op jit(solution)/shard_map/gather | solution.py:79
  384.1 9.3 %all-to-all-start.4 = ((f32[32,512,128]{2,1,0:T(8,128)}), f32[32,512,128]{2,1,0:T(8,128)}, u32[]{:S(2)}, u32[]{:S(2)}) async-start(f32[32,512,128]{2,1,0:T(8,128)} %bitcast.42), calls=%async_computation.4 | async-start | bytes 16777216 | tf_op jit(solution)/shard_map/all_to_all | solution.py:80
  393.5 54.4 %gather_fusion.2 = f32[16384,128]{1,0:T(8,128)} fusion(f32[2048,128]{1,0:T(8,128)S(1)} %get-tuple-element.17, s32[16384]{0:T(1024)S(1)} %get-tuple-element.18), kind=kCustom, calls=%fused_computation.2 | custom fusion | bytes 16842752 | tf_op jit(solution)/shard_map/gather | solution.py:78
  448.0 128.4 %all-to-all-done.4 = f32[32,512,128]{2,1,0:T(8,128)} async-done(((f32[32,512,128]{2,1,0:T(8,128)}), f32[32,512,128]{2,1,0:T(8,128)}, u32[]{:S(2)}, u32[]{:S(2)}) %all-to-all-start.4) | async-done | bytes 8388640 | tf_op jit(solution)/shard_map/all_to_all | solution.py:80
  576.3 8.0 %multiply_reduce_fusion = f32[32,512]{1,0:T(8,128)S(1)} fusion(f32[32,512,128]{2,1,0:T(8,128)} %all-to-all-done.4, f32[32,512,128]{2,1,0:T(8,128)} %bitcast.43), kind=kLoop, calls=%fused_computation.5 | loop fusion | flops 4177920 | bytes 16842752 | tf_op jit(solution)/shard_map/reduce_sum | solution.py:81
  584.4 90.5 %gather_fusion.3 = f32[16384]{0:T(1024)S(1)} fusion(f32[16384]{0:T(1024)S(1)} %bitcast.41, s32[16384]{0:T(1024)S(1)} %broadcast_clamp_fusion.1), kind=kCustom, calls=%fused_computation.3 | custom fusion | bytes 196608 | tf_op jit(solution)/shard_map/gather | solution.py:82
  674.9 1.6 reshape.242
  676.6 0.6 convert_element_type.47
  677.2 48.3 %reduce-scatter.2.cloned.1.call-done = f32[256,8]{1,0:T(8,128)} async-done(((f32[2048,8]{1,0:T(8,128)}), f32[256,8]{1,0:T(8,128)}) %reduce-scatter.2.cloned.1.call-update) | async-done | bytes 8208 | tf_op jit(solution)/shard_map/reduce_scatter | solution.py:83
  725.5 1.0 broadcast_multiply_fusion.2
  726.5 0.7 copy.43
  (39 shorter events, 1.3 us)
Async XLA Ops:
  10.4 94.6 %all-to-all-start.2 = ((f32[32,1,2]{2,1,0:T(1,128)}), f32[32,1,2]{2,1,0:T(1,128)S(1)}, u32[]{:S(2)}, u32[]{:S(2)}) async-start(f32[32,1,2]{2,1,0:T(1,128)} %copy.34), calls=%async_computation.2 | async-start | bytes 32768 | tf_op jit(solution)/shard_map/all_to_all | solution.py:40
  24.0 2.9 copy-start.2
  25.5 1.7 copy-start.1
  41.5 62.0 %copy-start.4 = (s32[16]{0:T(128)S(1)}, s32[16]{0:T(128)}, u32[]{:S(2)}) copy-start(s32[16]{0:T(128)} %param.7) | copy-start | bytes 196
  41.5 62.1 %copy-start.3 = (s32[2048]{0:T(1024)S(1)}, s32[2048]{0:T(1024)}, u32[]{:S(2)}) copy-start(s32[2048]{0:T(1024)} %param.6) | copy-start | bytes 24580
  105.0 172.0 %all-to-all-start = ((f32[32,1,2]{2,1,0:T(1,128)}), f32[32,1,2]{2,1,0:T(1,128)S(1)}, u32[]{:S(2)}, u32[]{:S(2)}) async-start(f32[32,1,2]{2,1,0:T(1,128)} %bitcast.2), calls=%async_computation | async-start | bytes 32768 | tf_op jit(solution)/shard_map/all_to_all | solution.py:39
  277.0 18.0 %all-to-all-start.1 = ((f32[32,2,128]{2,1,0:T(2,128)}), f32[32,2,128]{2,1,0:T(2,128)S(1)}, u32[]{:S(2)}, u32[]{:S(2)}) async-start(f32[32,2,128]{2,1,0:T(2,128)} %copy.33), calls=%async_computation.1 | async-start | bytes 65536 | tf_op jit(solution)/shard_map/all_to_all | solution.py:38
  295.1 34.6 %all-to-all-start.3 = ((s32[32,1,512]{2,1,0:T(1,128)}), s32[32,1,512]{2,1,0:T(1,128)S(1)}, u32[]{:S(2)}, u32[]{:S(2)}) async-start(s32[32,1,512]{2,1,0:T(1,128)} %bitcast.14), calls=%async_computation.3 | async-start | bytes 131072 | tf_op jit(solution)/shard_map/all_to_all | solution.py:79
  329.6 54.5 %copy-start = (f32[3136,128]{1,0:T(8,128)}, f32[3136,128]{1,0:T(8,128)S(1)}, u32[]{:S(2)}) copy-start(f32[3136,128]{1,0:T(8,128)S(1)} %multiply_select_fusion) | copy-start | bytes 4816900
  384.1 192.2 %all-to-all-start.4 = ((f32[32,512,128]{2,1,0:T(8,128)}), f32[32,512,128]{2,1,0:T(8,128)}, u32[]{:S(2)}, u32[]{:S(2)}) async-start(f32[32,512,128]{2,1,0:T(8,128)} %bitcast.42), calls=%async_computation.4 | async-start | bytes 16777216 | tf_op jit(solution)/shard_map/all_to_all | solution.py:80
  393.5 332.0 %reduce-scatter.2.cloned.1.call-start = ((), (), s32[]{:S(2)}) async-start(), calls=%async_computation.6 | async-start | bytes 1179648 | tf_op jit(solution)/shard_map/reduce_scatter | solution.py:83
Sparse Core Ops, SparseCore 0:
  676.6 48.8 reduce-scatter.1
where the time goes:
time: 736 us; the launch traced here: 734 us
  local copies, waits for them, and re-layouts  429 us (58%)
  waiting for transfers between devices  184 us (25%)
  starting transfers between devices  43.9 us (6%)
  blocking collectives  38 us (5%)
  other arithmetic  20.2 us (3%)
  between operations  14.4 us (2%)
    gather x1, local copies, waits for them, and re-layouts, on_device(): (flat_ids - cand_owner * per_owner)[ordering].reshape(owners, per_peer)  160 us
    all_to_all x1, waiting for transfers between devices, on_device(): lax.all_to_all(picked, 'doc', split_axis=0, concat_axis=0, tiled=True)  128 us
    gather x1, local copies, waits for them, and re-layouts, on_device(): products = sorted_dots[position].reshape(row_count, cand_count)  90.5 us
    scatter x1, local copies, waits for them, and re-layouts, on_device(): jnp.zeros((total_ids,), jnp.int32).at[position]  60.3 us
    gather x1, local copies, waits for them, and re-layouts, on_device(): own_rows = unit_rows[source_row].reshape(owners, per_peer, feat_width)  54.4 us
    gather x1, local copies, waits for them, and re-layouts, on_device(): centroids[lax.all_to_all(sorted_ids, 'doc', split_axis=0, concat_axis=0,...  54.4 us
    reduce_scatter x1, waiting for transfers between devices, on_device(): shared = lax.psum_scatter(products, 'cent', scatter_dimension=0, tiled=True)  48.3 us
    psum x1, blocking collectives, on_device(): cent_squares = lax.psum(jnp.sum(member_sums * member_sums, axis=1), 'cent')  24.9 us
  transfers between devices with their start and end apart: 6, of which 3 were waited for; matrix products, arithmetic and copies ran while one was open for 40% of the time, Pallas kernels for 0%

commit v1 on v0

v1 whole, which is shorter than its diff:
```python
import functools

import jax
import jax.numpy as jnp
from jax import lax
from jax.experimental import pallas as pl
from jax.experimental.pallas import tpu as pltpu
from jax.sharding import PartitionSpec as P

MESH = pl.DeviceIdType.MESH
F32, BF16, I32 = jnp.float32, jnp.bfloat16, jnp.int32
Z_CHIPS = 8
LANES = 128
SLOTS = 64
EXACT = lax.Precision.HIGHEST
NT = (((1,), (1,)), ((), ()))


def iota(shape, dim):
    return lax.broadcasted_iota(I32, shape, dim)


def split3(v):
    a = v.astype(BF16)
    rest = v - a.astype(F32)
    b = rest.astype(BF16)
    return a, b, (rest - b.astype(F32)).astype(BF16)


def kernel(
    nd, nz, nc,
    emb, old, live_in, cand, blk,
    ms, cnt, cen, cos,
    dr, dl, dmid, tr, tl, own_tab, tmid, trp, tlp,
    sq_src, sq_buf, scale, bsum, bcnt, pos, loc_hi, loc_lo, hi_ref, lo_ref,
    msgs, rbuf, sq2_src, sq2_buf, rhs, psend, pbuf, lsend, lbuf, srow, sloc,
    stage, part, s1buf, full, tbuf,
    zr_s, zr_r, zl_s, zl_r, xr_s, xr_r, xl_s, xl_r,
    sq_s, sq_r, sq2_s, sq2_r, a2a_s, a2a_r, p_s, p_r, l_s, l_r, sm_sem, s1_s, s1_r, t_s, t_r,
):
    nx = nd // nz
    rows, owned = emb.shape[0], old.shape[0]
    blocks = blk.shape[0]
    me = lax.axis_index("doc")
    c = lax.axis_index("cent")
    x, z = me // nz, me % nz
    per_z = pos.shape[0] * LANES // nz
    lrows = per_z // LANES
    per_owner = per_z // nx
    urows = lrows // nx

    def copy(src, dst, ssem, rsem, doc, cent):
        return pltpu.make_async_remote_copy(
            src_ref=src, dst_ref=dst, send_sem=ssem, recv_sem=rsem,
            device_id=(doc, cent), device_id_type=MESH,
        )

    bar = pltpu.get_barrier_semaphore()

    def greet(doc, cent):
        pl.semaphore_signal(bar, inc=1, device_id=(doc, cent), device_id_type=MESH)

    lax.fori_loop(1, nd, lambda k, _: (greet((me + k) % nd, c), 0)[1], 0)
    lax.fori_loop(1, nc, lambda k, _: (greet(me, (c + k) % nc), 0)[1], 0)

    @pl.when(c != z)
    def _():
        lax.fori_loop(1, nz, lambda k, _: (greet(x * nz + (z + k) % nz, z), 0)[1], 0)
        pl.semaphore_wait(bar, nd - 1 + nc - 1 + nz - 1)

    @pl.when(c == z)
    def _():
        pl.semaphore_wait(bar, nd - 1 + nc - 1)

    def ring(n, own, right, left, mid, rs, rr, ls, lr, right_id, left_id):
        half = own.shape[0] // 2
        last = n // 2
        out_r, out_l = {}, {}
        for s in range(1, last + 1):
            src_r = own if s == 1 else right[s - 2]
            src_l = own if s == 1 else left[s - 2]
            for h in (0, 1):
                cut = pl.ds(h * half, half)
                if s < last or h == 0:
                    dst = (right[s - 1] if s < last else mid).at[cut]
                    out_r[s, h] = copy(src_r.at[cut], dst, rs.at[s - 1, h], rr.at[s - 1, h], right_id, c)
                if s < last or h == 1:
                    dst = (left[s - 1] if s < last else mid).at[cut]
                    out_l[s, h] = copy(src_l.at[cut], dst, ls.at[s - 1, h], lr.at[s - 1, h], left_id, c)
        return out_r, out_l

    zr, zl = ring(nz, emb, dr, dl, dmid, zr_s, zr_r, zl_s, zl_r,
                  x * nz + (z + 1) % nz, x * nz + (z + nz - 1) % nz)
    xr, xl = ring(nx, old, tr, tl, tmid, xr_s, xr_r, xl_s, xl_r,
                  (x + 1) % nx * nz + z, (x + nx - 1) % nx * nz + z)

    def forward(right, left, s, h):
        right[s, h].wait_recv()
        if (s + 1, h) in right:
            right[s + 1, h].start()
        left[s, 1 - h].wait_recv()
        if (s + 1, 1 - h) in left:
            left[s + 1, 1 - h].start()

    zr[1, 0].start()
    zl[1, 1].start()
    xr[1, 0].start()
    xl[1, 1].start()
    zr[1, 1].start()
    zl[1, 0].start()
    xr[1, 1].start()
    xl[1, 0].start()

    def cent_copy(src, buf, ss, rs, k):
        return copy(src, buf.at[c], ss.at[k], rs.at[c], me, (c + k) % nc)

    def cent_start(src, buf, ss, rs):
        lax.fori_loop(1, nc, lambda k, _: (cent_copy(src, buf, ss, rs, k).start(), 0)[1], 0)
        buf[c] = src[...]

    def cent_wait(src, buf, ss, rs):
        def body(k, _):
            other = (c + k) % nc
            copy(src, buf.at[other], ss.at[k], rs.at[other], me, other).wait()
            return 0
        lax.fori_loop(1, nc, body, 0)

    def cross_copy(src, dst, ss, rs, k):
        return copy(src, dst(z), ss.at[k], rs.at[z], x * nz + c, (c + k) % nc)

    def cross_start(src, dst, ss, rs):
        lax.fori_loop(1, nc, lambda k, _: (cross_copy(src, dst, ss, rs, k).start(), 0)[1], 0)

        @pl.when(c != z)
        def _():
            cross_copy(src, dst, ss, rs, 0).start()

        @pl.when(c == z)
        def _():
            dst(z)[...] = src[...]

    def cross_wait(src, dst, ss, rs):
        def body(k, _):
            other = (z + k) % nz
            copy(src, dst(other), ss.at[k], rs.at[other], x * nz + c, (c + k) % nc).wait()
            return 0
        lax.fori_loop(1, nz, body, 0)

        @pl.when(c != z)
        def _():
            cross_copy(src, dst, ss, rs, 0).wait()

    for table in (own_tab, tmid, trp, tlp):
        table[owned:, :] = jnp.zeros((table.shape[0] - owned, LANES), F32)

    def squares(b, _):
        t = emb[pl.ds(pl.multiple_of(b * LANES, LANES), LANES), :].T
        sq_src[pl.ds(b, 1), :] = jnp.sum(t * t, axis=0, keepdims=True)
        return 0

    lax.fori_loop(0, rows // LANES, squares, 0)
    cent_start(sq_src, sq_buf, sq_s, sq_r)

    ids = jnp.concatenate([cand[:, LANES * i:LANES * (i + 1)] for i in range(rows // LANES)], 0).astype(F32)
    qrows = ids.shape[0]
    owner = jnp.floor((ids + 0.5) * (1.0 / owned))
    loc = ids - owner * owned
    loc_top = jnp.floor(loc * (1.0 / LANES))
    loc_hi[...] = loc_top
    loc_lo[...] = loc - loc_top * LANES
    upper = (iota((LANES, LANES), 0) < iota((LANES, LANES), 1)).astype(F32)
    upper_ones = jnp.concatenate([upper, jnp.ones((LANES, LANES), F32)], 1).astype(BF16)
    lower = (iota((qrows, qrows), 0) > iota((qrows, qrows), 1)).astype(F32).astype(BF16)
    pos[...] = jnp.zeros_like(pos)

    def place(m, _):
        mask = (owner == m.astype(F32)).astype(F32)
        counted = jnp.dot(mask.astype(BF16), upper_ones, preferred_element_type=F32)
        above = jnp.dot(lower, counted[:, LANES:].astype(BF16), preferred_element_type=F32)
        base = ((m % nz) * per_z + (m // nz) * per_owner).astype(F32)
        pos[...] += mask * (counted[:, :LANES] + above + base)
        return 0

    lax.fori_loop(0, nd, place, 0)
    top = jnp.floor(pos[...] * (1.0 / LANES))
    hi_ref[...] = top
    lo_ref[...] = pos[...] - top * LANES

    shift = (c * lrows).astype(F32)
    lane_row = iota((1, LANES), 1).astype(F32)

    def lists(i, acc):
        left_parts, right_parts = [], []
        for j in range(8):
            q = pl.ds(i * 8 + j, 1)
            at = (iota((lrows, LANES), 0).astype(F32) == hi_ref[q, :] - shift).astype(F32)
            left_parts.append(jnp.concatenate(
                [at * i.astype(F32), at * lane_row, at * loc_hi[q, :], at * loc_lo[q, :]], 0).astype(BF16))
            right_parts.append(
                (iota((LANES, LANES), 0).astype(F32) == lo_ref[q, :]).astype(F32).astype(BF16))
        return acc + lax.dot_general(
            jnp.concatenate(left_parts, 1), jnp.concatenate(right_parts, 1), NT, preferred_element_type=F32)

    found = lax.fori_loop(0, qrows // 8, lists, jnp.zeros((4 * lrows, LANES), F32))
    lsend[0] = (found[:lrows] * LANES + found[lrows:2 * lrows]).astype(I32)
    lsend[1] = (found[2 * lrows:3 * lrows] * LANES + found[3 * lrows:]).astype(I32)
    lists_at = lambda s: lbuf.at[s]
    cross_start(lsend, lists_at, l_s, l_r)

    cent_wait(sq_src, sq_buf, sq_s, sq_r)
    total = sq_buf[0]
    for k in range(1, nc):
        total = total + sq_buf[k]
    alive = live_in[...].astype(F32)
    scale[...] = lax.rsqrt(total + 1e-6) * alive

    def block_sum(b, acc):
        weight = jnp.where(iota((blocks, LANES), 0) == b, scale[...], 0.0)
        return acc + jnp.dot(weight, emb[pl.ds(pl.multiple_of(b * LANES, LANES), LANES), :],
                             precision=EXACT, preferred_element_type=F32)

    bsum[...] = lax.fori_loop(0, blocks, block_sum, jnp.zeros((blocks, LANES), F32))
    bcnt[...] = jnp.broadcast_to(jnp.sum(alive, axis=1, keepdims=True), (blocks, LANES))
    owners = [blk[b] // owned for b in range(blocks)]
    place_of = [jnp.int32(0)] + [
        jnp.where(owners[b] == owners[b - 1], 1, 0) for b in range(1, blocks)]
    local = [(blk[b] - owners[b] * owned).astype(F32) for b in range(blocks)]

    def message(o, _):
        tile = jnp.zeros((8, LANES), F32)
        line = iota((8, LANES), 0)
        for b in range(blocks):
            at = jnp.where(owners[b] == o, place_of[b], -8)
            tile = jnp.where(line == at, bsum[b:b + 1, :], tile)
            tile = jnp.where(line == at + 2, local[b], tile)
            tile = jnp.where(line == at + 4, bcnt[b:b + 1, :], tile)
        msgs[o] = tile
        return 0

    lax.fori_loop(0, nd, message, 0)

    def a2a_start(k, _):
        to = (me + k) % nd
        copy(msgs.at[to], rbuf.at[me], a2a_s.at[k], a2a_r.at[me], to, c).start()
        return 0

    def a2a_wait(k, _):
        other = (me + k) % nd
        copy(msgs.at[other], rbuf.at[other], a2a_s.at[k], a2a_r.at[other], other, c).wait()
        return 0

    lax.fori_loop(1, nd, a2a_start, 0)
    rbuf[me] = msgs[me]
    forward(zr, zl, 1, 0)
    lax.fori_loop(1, nd, a2a_wait, 0)

    def slots(first, empty):
        return jnp.concatenate(
            [rbuf[:, first, :], rbuf[:, first + 1, :],
             jnp.full((LANES - 2 * nd, LANES), empty, F32)], 0)

    sums, slot_ids, slot_counts = slots(0, 0.0), slots(2, -1.0), slots(4, 0.0)
    slot_ids = jnp.where(slot_counts > 0, slot_ids, -1.0)
    ids_lane = slot_ids.T
    same = jnp.where((slot_ids == ids_lane) & (slot_counts > 0), 1.0, 0.0)
    group = jnp.dot(same, sums, precision=EXACT, preferred_element_type=F32)
    square = group * group
    sq2_src[...] = jnp.broadcast_to(jnp.sum(square.T, axis=0, keepdims=True), (8, LANES))
    cent_start(sq2_src, sq2_buf, sq2_s, sq2_r)

    earlier = jnp.sum(
        jnp.where(iota((LANES, LANES), 0) < iota((LANES, LANES), 1), same, 0.0), axis=0, keepdims=True)
    first_ids = jnp.where(earlier > 0, -1.0, ids_lane[0:1])
    counts_lane = slot_counts.T[0:1]
    ids_top = jnp.floor(ids_lane[0:1] * (1.0 / LANES))
    ids_low = ids_lane[0:1] - ids_top * LANES
    count_left = jnp.where(iota(cnt.shape, 0).astype(F32) == ids_top, counts_lane, 0.0).astype(BF16)
    count_right = (iota((LANES, LANES), 0).astype(F32) == ids_low).astype(F32).astype(BF16)
    cnt[...] = lax.dot_general(count_left, count_right, NT, preferred_element_type=F32).astype(I32)

    cent_wait(sq2_src, sq2_buf, sq2_s, sq2_r)
    total2 = sq2_buf[0]
    for k in range(1, nc):
        total2 = total2 + sq2_buf[k]
    inverse = lax.rsqrt(jnp.broadcast_to(total2[0:1], (LANES, LANES)) + 1e-6).T
    normal = group * inverse
    psend[0:SLOTS, :] = normal[:SLOTS]
    psend[SLOTS:SLOTS + 8, :] = jnp.broadcast_to(first_ids, (8, LANES))

    def patch_copy(k):
        return copy(psend, pbuf.at[k - 1], p_s.at[k - 1], p_r.at[k - 1], (x + k) % nx * nz + z, c)

    for k in range(1, nx):
        patch_copy(k).start()

    ones = jnp.ones((LANES, LANES), BF16)
    rhs[...] = jnp.concatenate([*split3(normal), ones, *split3(group)], 1)
    step = owned // 7

    def picked(i, chosen, width):
        hit = (iota((step, LANES), 0) + i * step).astype(F32) == chosen
        return jnp.dot(hit.astype(F32).astype(BF16), rhs[:, :width], preferred_element_type=F32)

    def patched(out, before):
        new = out[:, :LANES] + out[:, LANES:2 * LANES] + out[:, 2 * LANES:3 * LANES]
        return jnp.where(out[:, 3 * LANES:4 * LANES] > 0, new, before)

    def cut(i):
        return pl.ds(pl.multiple_of(i * step, 8), step)

    def own_table(i, _):
        out = picked(i, first_ids, 7 * LANES)
        ms[cut(i), :] = out[:, 4 * LANES:5 * LANES] + out[:, 5 * LANES:6 * LANES] + out[:, 6 * LANES:]
        new = patched(out, old[cut(i), :])
        cen[cut(i), :] = new
        own_tab[cut(i), :] = new
        return 0

    lax.fori_loop(0, 7, own_table, 0)
    forward(xr, xl, 1, 0)
    forward(zr, zl, 1, 1)

    cross_wait(lsend, lists_at, l_s, l_r)
    order = [0] + [d * s for d in range(1, nz // 2) for s in (-1, 1)] + [nz // 2]
    source = [(z + nz + d) % nz for d in order]
    for i in range(nz):
        here = pl.ds(i * lrows, lrows)
        pltpu.make_async_copy(lbuf.at[source[i], 0], srow.at[here], sm_sem.at[0, i]).start()
        pltpu.make_async_copy(lbuf.at[source[i], 1], sloc.at[here], sm_sem.at[1, i]).start()
    for i in range(nz):
        here = pl.ds(i * lrows, lrows)
        pltpu.make_async_copy(lbuf.at[source[i], 0], srow.at[here], sm_sem.at[0, i]).wait()
        pltpu.make_async_copy(lbuf.at[source[i], 1], sloc.at[here], sm_sem.at[1, i]).wait()

    documents = {0: emb, nz // 2: dmid}
    for d in range(1, nz // 2):
        documents[-d], documents[d] = dr[d - 1], dl[d - 1]
    tables = {0: own_tab, -1: trp, 1: tlp, 2: tmid}

    def dots(distance, dx):
        docs, table = documents[distance], tables[dx]
        first = order.index(distance) * lrows
        at = (x + nx + dx) % nx * urows

        def body(i, _):
            line = first + at + i
            for q in range(0, LANES, 8):
                stage[pl.ds(q, 8), :] = jnp.concatenate(
                    [docs[pl.ds(srow[line, u] & (rows - 1), 1), :]
                     * table[pl.ds(sloc[line, u] & (table.shape[0] - 1), 1), :]
                     for u in range(q, q + 8)], 0)
            part[pl.ds(line, 1), :] = jnp.sum(stage[...].T, axis=0, keepdims=True)
            return 0

        lax.fori_loop(0, urows, body, 0)

    def part_copy(i):
        return copy(part.at[pl.ds(i * lrows, lrows)], s1buf.at[c], s1_s.at[i], s1_r.at[c], me, source[i])

    def hand_on(distance):
        i = order.index(distance)

        @pl.when(source[i] != c)
        def _():
            part_copy(i).start()

        @pl.when(source[i] == c)
        def _():
            s1buf[c] = part[pl.ds(i * lrows, lrows), :]

    def patch(k, before, after):
        patch_copy(k).wait_recv()
        new = pbuf[k - 1]
        rhs[0:SLOTS, 0:3 * LANES] = jnp.concatenate(split3(new[:SLOTS]), 1)
        chosen = new[SLOTS:SLOTS + 1]

        def body(i, _):
            after[cut(i), :] = patched(picked(i, chosen, 4 * LANES), before[cut(i), :])
            return 0

        lax.fori_loop(0, 7, body, 0)

    for d in (0, -1, 1):
        dots(d, 0)
    forward(zr, zl, 2, 0)
    xr[1, 1].wait_recv()
    xl[1, 0].wait_recv()
    patch(1, tr[0], trp)
    patch(3, tl[0], tlp)
    for d in (0, -1, 1):
        dots(d, -1)
        dots(d, 1)
    forward(zr, zl, 2, 1)
    for d in (-2, 2):
        for dx in (0, -1, 1):
            dots(d, dx)
    forward(zr, zl, 3, 0)
    xr[2, 0].wait_recv()
    xl[2, 1].wait_recv()
    patch(2, tmid, tmid)
    for d in (0, -1, 1, -2, 2):
        dots(d, 2)
        hand_on(d)
    forward(zr, zl, 3, 1)
    for d in (-3, 3):
        for dx in (0, -1, 1, 2):
            dots(d, dx)
        hand_on(d)
    zr[4, 0].wait_recv()
    zl[4, 1].wait_recv()
    for dx in (0, -1, 1, 2):
        dots(4, dx)
    hand_on(4)

    def part_wait(k, _):
        other = (c + k) % nc
        copy(full, s1buf.at[other], s1_s.at[0], s1_r.at[other], me, other).wait_recv()
        return 0

    lax.fori_loop(1, nc, part_wait, 0)
    total3 = s1buf[0]
    for k in range(1, nc):
        total3 = total3 + s1buf[k]
    full[...] = total3
    sums_at = lambda s: tbuf.at[pl.ds(pl.multiple_of(s * lrows, 8), lrows)]
    cross_start(full, sums_at, t_s, t_r)
    cross_wait(full, sums_at, t_s, t_r)

    table = jnp.concatenate(split3(tbuf[...]), 0)
    share = qrows // nc
    for g in range(share // 8):
        lows = [lo_ref[pl.ds(c * share + g * 8 + j, 1), :] for j in range(8)]
        tops = [hi_ref[pl.ds(c * share + g * 8 + j, 1), :] for j in range(8)]
        sel = jnp.concatenate(
            [(iota((LANES, LANES), 0).astype(F32) == v).astype(F32).astype(BF16) for v in lows], 1)
        got = jnp.dot(table, sel, preferred_element_type=F32)
        got = got[:qrows] + got[qrows:2 * qrows] + got[2 * qrows:]
        top_all = jnp.concatenate(tops, 1)
        line = jnp.sum(
            jnp.where(iota(got.shape, 0).astype(F32) == top_all, got, 0.0), axis=0, keepdims=True)
        factor = scale[pl.ds(c * (share // 8) + g, 1), :]
        for j in range(8):
            cos[j:j + 1, g * LANES:(g + 1) * LANES] = line[:, j * LANES:(j + 1) * LANES] * factor

    for ring_copies in (zr, zl, xr, xl):
        for one in ring_copies.values():
            one.wait_send()
    for k in range(1, nx):
        patch_copy(k).wait_send()
    for i in range(nz):
        @pl.when(source[i] != c)
        def _(i=i):
            part_copy(i).wait_send()


def on_device(nd, nc, embeddings, row_mask, block_cluster, candidates, old_centroids):
    rows, width = embeddings.shape
    owned = old_centroids.shape[0]
    nz = Z_CHIPS
    nx = nd // nz
    cands = candidates.shape[1]
    blocks = block_cluster.shape[0]
    qrows = rows * cands // LANES
    lrows = qrows // nz
    table_rows = 1 << (owned - 1).bit_length()
    vmem = lambda *s: pltpu.VMEM(s, F32)
    dma = lambda *s: pltpu.SemaphoreType.DMA(s)
    in_vmem = pl.BlockSpec(memory_space=pltpu.VMEM)
    scratch = [
        [vmem(rows, width)] * (nz // 2 - 1), [vmem(rows, width)] * (nz // 2 - 1), vmem(rows, width),
        [vmem(owned, width)], [vmem(owned, width)], *[vmem(table_rows, width)] * 4,
        vmem(blocks, LANES), vmem(nc, blocks, LANES), vmem(blocks, LANES),
        vmem(blocks, LANES), vmem(blocks, LANES),
        vmem(qrows, LANES), vmem(qrows, LANES), vmem(qrows, LANES), vmem(qrows, LANES), vmem(qrows, LANES),
        vmem(nd, 8, LANES), vmem(nd, 8, LANES), vmem(8, LANES), vmem(nc, 8, LANES),
        pltpu.VMEM((LANES, 7 * LANES), BF16), vmem(SLOTS + 8, LANES), vmem(nx - 1, SLOTS + 8, LANES),
        pltpu.VMEM((2, lrows, LANES), I32), pltpu.VMEM((nz, 2, lrows, LANES), I32),
        pltpu.SMEM((qrows, LANES), I32), pltpu.SMEM((qrows, LANES), I32),
        vmem(LANES, LANES), vmem(qrows, LANES), vmem(nc, lrows, LANES), vmem(lrows, LANES), vmem(qrows, LANES),
        dma(nz // 2, 2), dma(nz // 2, 2), dma(nz // 2, 2), dma(nz // 2, 2),
        dma(nx // 2, 2), dma(nx // 2, 2), dma(nx // 2, 2), dma(nx // 2, 2),
        dma(nc), dma(nc), dma(nc), dma(nc), dma(nd), dma(nd), dma(nx - 1), dma(nx - 1),
        dma(nc), dma(nz), dma(2, nz), dma(nz), dma(nc), dma(nc), dma(nz),
    ]
    sums, counts, cents, cosines = pl.pallas_call(
        functools.partial(kernel, nd, nz, nc),
        out_shape=(
            jax.ShapeDtypeStruct((owned, width), F32),
            jax.ShapeDtypeStruct((-(-owned // (8 * LANES)) * 8, LANES), I32),
            jax.ShapeDtypeStruct((owned, width), F32),
            jax.ShapeDtypeStruct((cands, rows // nc), F32),
        ),
        in_specs=[in_vmem] * 4 + [pl.BlockSpec(memory_space=pltpu.SMEM)],
        out_specs=(in_vmem,) * 4,
        scratch_shapes=scratch,
        compiler_params=pltpu.CompilerParams(
            collective_id=0, has_side_effects=True, vmem_limit_bytes=52 << 20),
        name="update",
    )(embeddings, old_centroids, row_mask.reshape(blocks, rows // blocks), candidates.T, block_cluster)
    return sums, counts.reshape(-1)[:owned], cents, cosines.T


def solution(mesh):
    placed = (P("doc", "cent"), P("doc"), P("doc"), P("doc", None), P("doc", "cent"))
    return jax.shard_map(
        functools.partial(on_device, mesh.shape["doc"], mesh.shape["cent"]),
        mesh=mesh,
        in_specs=placed,
        out_specs=(P("doc", "cent"), P("doc"), P("doc", "cent"), P(("doc", "cent"), None)),
        check_vma=False,
    )
```

time: 736 us -> 133 us (0.18)
  local copies, waits for them, and re-layouts: 429 us -> 8.56 us
  waiting for transfers between devices: 184 us -> 0 us
  Pallas kernels: 0 us -> 123 us
  starting transfers between devices: 43.9 us -> 0 us
  blocking collectives: 38 us -> 0 us
  other arithmetic: 20.2 us -> 0 us
  between operations: 14.4 us -> 0.66 us
    gather x4 -> x0, local copies, waits for them, and re-layouts: 360 us -> none  [the longest x1 160 us: on_device(): (flat_ids - cand_owner * per_owner)[ordering].reshape(owners, per_peer)]
    all_to_all x5 -> x0, waiting for transfers between devices: 136 us -> none  [the longest x1 128 us: on_device(): lax.all_to_all(picked, 'doc', split_axis=0, concat_axis=0, tiled=True)]
    pallas_call x0 -> x1, Pallas kernels: none -> 123 us  [on_device(): pl.pallas_call(functools.partial(kernel, nd, nz, nc), out_shape=(jax.Shap...]
    scatter x1 -> x0, local copies, waits for them, and re-layouts: 60.3 us -> none  [on_device(): jnp.zeros((total_ids,), jnp.int32).at[position]]
    reduce_scatter x1 -> x0, waiting for transfers between devices: 48.3 us -> none  [on_device(): shared = lax.psum_scatter(products, 'cent', scatter_dimension=0, tiled=True)]
    all_to_all x5 -> x0, starting transfers between devices: 43.8 us -> none  [the longest x1 11.9 us: on_device(): lax.all_to_all(slot_counts, 'doc', split_axis=0, concat_axis=0, tiled=True)]
    psum x2 -> x0, blocking collectives: 38 us -> none  [the longest x1 24.9 us: on_device(): cent_squares = lax.psum(jnp.sum(member_sums * member_sums, axis=1), 'cent')]
    reduce_sum x6 -> x0, other arithmetic: 10.3 us -> none  [the longest x1 8 us: on_device(): sorted_dots = jnp.sum(vectors * own_rows, axis=-1).reshape(-1)]
  transfers between devices with their start and end apart: 6 -> 0, of which waited for: 3 -> 0; matrix products, arithmetic and copies ran while one was open for 40% -> 0% of each run, Pallas kernels for 0% -> 0%
where the time goes in v1:
time: 133 us
  Pallas kernels  123 us (92%)
  local copies, waits for them, and re-layouts  8.56 us (6%)
    pallas_call x1, Pallas kernels, on_device(): pl.pallas_call(functools.partial(kernel, nd, nz, nc), out_shape=(jax.Shap...  123 us
    unnamed x14, local copies, waits for them, and re-layouts  8.56 us

profile of v1, /device:TPU:1, one launch (start us, length us, event | category | flops | bytes accessed | tf_op | source)
XLA Modules:
  0.0 132.5 jit_solution(13737380995963525870)
XLA Ops:
  0.6 0.0 copy-start
  0.6 1.2 copy-done
  1.9 0.0 copy-start.1
  1.9 0.8 copy-done.1
  2.7 0.0 copy-start.2
  2.7 0.7 copy-done.2
  3.4 0.0 copy-start.3
  3.4 0.7 copy-done.3
  4.1 123.3 %update.1 = (f32[3136,128]{1,0:T(8,128)}, s32[32,128]{1,0:T(8,128)S(1)}, f32[3136,128]{1,0:T(8,128)}, f32[8,256]{1,0:T(8,128)S(1)}) custom-call(f32[2048,128]{1,0:T(8,128)S(1)} %copy-done, f32[3136,128]{1,0:T(8,128)} %old.1, s32[16,128]{1,0:T(8,128)S(1)} %bitcast.7, s32[8,2048]{1,0:T(8,128)S(1)} %bitcast.5, s32[16]{0:T(128)S(1)} %copy-done.3), custom_call_target="tpu_custom_call" | custom-call | tf_op jit(solution)/shard_map/update/pallas_call | solution.py:485
  127.4 0.0 copy-start.4
  127.4 2.8 %copy.13 = f32[3136,128]{1,0:T(8,128)} copy(f32[3136,128]{1,0:T(8,128)} %get-tuple-element.16) | data formatting | bytes 3211264
  130.2 0.6 copy.14
  130.8 0.0 copy-done.4
  130.8 1.2 copy.15
  131.9 0.6 copy.16
Async XLA Ops:
  0.6 1.2 copy-start
  1.9 0.8 copy-start.1
  2.7 0.7 copy-start.2
  3.4 0.7 copy-start.3
  127.4 3.4 %copy-start.4 = (f32[3136,128]{1,0:T(8,128)S(1)}, f32[3136,128]{1,0:T(8,128)}, u32[]{:S(2)}) copy-start(f32[3136,128]{1,0:T(8,128)} %get-tuple-element.18) | copy-start | bytes 4816900

commit v2 on v1

--- a/solution.py
+++ b/solution.py
@@ -12,12 +12,16 @@
 Z_CHIPS = 8
 LANES = 128
 SLOTS = 64
-EXACT = lax.Precision.HIGHEST
 NT = (((1,), (1,)), ((), ()))
 
 
 def iota(shape, dim):
     return lax.broadcasted_iota(I32, shape, dim)
+
+
+def split2(v):
+    a = v.astype(BF16)
+    return a, (v - a.astype(F32)).astype(BF16)
 
 
 def split3(v):
@@ -27,19 +31,60 @@
     return a, b, (rest - b.astype(F32)).astype(BF16)
 
 
+def rhs_of(values):
+    return jnp.concatenate([values, jnp.ones((2 * LANES, LANES), BF16)], 1)
+
+
+def one_hot(chosen, first, step):
+    hit = (iota((step, LANES), 0) + first).astype(F32) == chosen
+    return hit.astype(F32).astype(BF16)
+
+
+def replaced(chosen, rhs, first, before):
+    hit = one_hot(chosen, first, before.shape[0])
+    out = jnp.dot(jnp.concatenate([hit, hit], 1), rhs, preferred_element_type=F32)
+    return jnp.where(out[:, LANES:] > 0, out[:, :LANES], before)
+
+
+def expand(slots, old, ms, cnt, cen):
+    step = ms.shape[0]
+    i = pl.program_id(0)
+    empty = jnp.zeros((LANES - SLOTS, LANES), BF16)
+    parts = [split2(slots[k * SLOTS:(k + 1) * SLOTS, :]) for k in (0, 1)]
+    rhs = jnp.concatenate([jnp.concatenate([p[k] if j == 0 else empty for k in (0, 1) for j in (0, 1)], 0)
+                           for p in parts], 1)
+    chosen = slots[2 * SLOTS:2 * SLOTS + 1, :]
+    hit = one_hot(chosen, i * step, step)
+    twice = jnp.concatenate([hit, hit], 1)
+    out = jnp.dot(twice, jnp.concatenate([rhs, jnp.ones((2 * LANES, LANES), BF16)], 1),
+                  preferred_element_type=F32)
+    ms[...] = out[:, :LANES]
+    cen[...] = jnp.where(out[:, 2 * LANES:] > 0, out[:, LANES:2 * LANES], old[...])
+
+    @pl.when(i == 0)
+    def _():
+        ids = slots[2 * SLOTS + 8:2 * SLOTS + 9, :]
+        ids_top = jnp.floor(ids * (1.0 / LANES))
+        count_left = jnp.where(iota(cnt.shape, 0).astype(F32) == ids_top,
+                               slots[2 * SLOTS + 16:2 * SLOTS + 17, :], 0.0).astype(BF16)
+        count_right = (iota((LANES, LANES), 0).astype(F32) == ids - ids_top * LANES).astype(F32).astype(BF16)
+        cnt[...] = lax.dot_general(count_left, count_right, NT, preferred_element_type=F32).astype(I32)
+
+
 def kernel(
     nd, nz, nc,
+    emb_in, old_in, live_hbm, cand_hbm, blk_hbm,
+    found_slots, cos,
     emb, old, live_in, cand, blk,
-    ms, cnt, cen, cos,
     dr, dl, dmid, tr, tl, own_tab, tmid, trp, tlp,
     sq_src, sq_buf, scale, bsum, bcnt, pos, loc_hi, loc_lo, hi_ref, lo_ref,
     msgs, rbuf, sq2_src, sq2_buf, rhs, psend, pbuf, lsend, lbuf, srow, sloc,
-    stage, part, s1buf, full, tbuf,
+    stage, part, s1buf, full, tbuf, sel,
     zr_s, zr_r, zl_s, zl_r, xr_s, xr_r, xl_s, xl_r,
-    sq_s, sq_r, sq2_s, sq2_r, a2a_s, a2a_r, p_s, p_r, l_s, l_r, sm_sem, s1_s, s1_r, t_s, t_r,
+    sq_s, sq_r, sq2_s, sq2_r, a2a_s, a2a_r, p_s, p_r, l_s, l_r, sm_sem, s1_s, s1_r, t_s, t_r, in_sem,
 ):
     nx = nd // nz
-    rows, owned = emb.shape[0], old.shape[0]
+    rows, owned = emb_in.shape[0], old_in.shape[0]
     blocks = blk.shape[0]
     me = lax.axis_index("doc")
     c = lax.axis_index("cent")
@@ -54,6 +99,11 @@
             src_ref=src, dst_ref=dst, send_sem=ssem, recv_sem=rsem,
             device_id=(doc, cent), device_id_type=MESH,
         )
+
+    loads = [pltpu.make_async_copy(a, b, in_sem.at[i]) for i, (a, b) in enumerate(
+        ((emb_in, emb), (cand_hbm, cand), (live_hbm, live_in), (blk_hbm, blk), (old_in, old)))]
+    for load in loads:
+        load.start()
 
     bar = pltpu.get_barrier_semaphore()
 
@@ -89,9 +139,9 @@
                     out_l[s, h] = copy(src_l.at[cut], dst, ls.at[s - 1, h], lr.at[s - 1, h], left_id, c)
         return out_r, out_l
 
-    zr, zl = ring(nz, emb, dr, dl, dmid, zr_s, zr_r, zl_s, zl_r,
+    zr, zl = ring(nz, emb_in, dr, dl, dmid, zr_s, zr_r, zl_s, zl_r,
                   x * nz + (z + 1) % nz, x * nz + (z + nz - 1) % nz)
-    xr, xl = ring(nx, old, tr, tl, tmid, xr_s, xr_r, xl_s, xl_r,
+    xr, xl = ring(nx, old_in, tr, tl, tmid, xr_s, xr_r, xl_s, xl_r,
                   (x + 1) % nx * nz + z, (x + nx - 1) % nx * nz + z)
 
     def forward(right, left, s, h):
@@ -106,10 +156,6 @@
     zl[1, 1].start()
     xr[1, 0].start()
     xl[1, 1].start()
-    zr[1, 1].start()
-    zl[1, 0].start()
-    xr[1, 1].start()
-    xl[1, 0].start()
 
     def cent_copy(src, buf, ss, rs, k):
         return copy(src, buf.at[c], ss.at[k], rs.at[c], me, (c + k) % nc)
@@ -153,13 +199,16 @@
     for table in (own_tab, tmid, trp, tlp):
         table[owned:, :] = jnp.zeros((table.shape[0] - owned, LANES), F32)
 
-    def squares(b, _):
-        t = emb[pl.ds(pl.multiple_of(b * LANES, LANES), LANES), :].T
-        sq_src[pl.ds(b, 1), :] = jnp.sum(t * t, axis=0, keepdims=True)
-        return 0
-
-    lax.fori_loop(0, rows // LANES, squares, 0)
+    for load in loads[:4]:
+        load.wait()
+    for b in range(blocks):
+        t = emb[b * LANES:(b + 1) * LANES, :].T
+        sq_src[b:b + 1, :] = jnp.sum(t * t, axis=0, keepdims=True)
     cent_start(sq_src, sq_buf, sq_s, sq_r)
+    zr[1, 1].start()
+    zl[1, 0].start()
+    xr[1, 1].start()
+    xl[1, 0].start()
 
     ids = jnp.concatenate([cand[:, LANES * i:LANES * (i + 1)] for i in range(rows // LANES)], 0).astype(F32)
     qrows = ids.shape[0]
@@ -168,44 +217,25 @@
     loc_top = jnp.floor(loc * (1.0 / LANES))
     loc_hi[...] = loc_top
     loc_lo[...] = loc - loc_top * LANES
-    upper = (iota((LANES, LANES), 0) < iota((LANES, LANES), 1)).astype(F32)
-    upper_ones = jnp.concatenate([upper, jnp.ones((LANES, LANES), F32)], 1).astype(BF16)
+    upper_ones = jnp.concatenate(
+        [(iota((LANES, LANES), 0) < iota((LANES, LANES), 1)).astype(F32), jnp.ones((LANES, LANES), F32)],
+        0).astype(BF16)
     lower = (iota((qrows, qrows), 0) > iota((qrows, qrows), 1)).astype(F32).astype(BF16)
-    pos[...] = jnp.zeros_like(pos)
-
-    def place(m, _):
-        mask = (owner == m.astype(F32)).astype(F32)
-        counted = jnp.dot(mask.astype(BF16), upper_ones, preferred_element_type=F32)
-        above = jnp.dot(lower, counted[:, LANES:].astype(BF16), preferred_element_type=F32)
-        base = ((m % nz) * per_z + (m // nz) * per_owner).astype(F32)
-        pos[...] += mask * (counted[:, :LANES] + above + base)
-        return 0
-
-    lax.fori_loop(0, nd, place, 0)
+    places = jnp.zeros((qrows, LANES), F32)
+    for first in range(0, nd, 8):
+        masks = [(owner == float(m)).astype(F32) for m in range(first, first + 8)]
+        coded = [v.astype(BF16) for v in masks]
+        above = jnp.dot(lower, jnp.concatenate(coded, 1), preferred_element_type=F32).astype(BF16)
+        both = jnp.concatenate(
+            [jnp.concatenate([coded[m], above[:, m * LANES:(m + 1) * LANES]], 1) for m in range(8)], 0)
+        rank = jnp.dot(both, upper_ones, preferred_element_type=F32)
+        for m in range(8):
+            start = float((first + m) % nz * per_z + (first + m) // nz * per_owner)
+            places = places + masks[m] * (rank[m * qrows:(m + 1) * qrows] + start)
+    pos[...] = places
     top = jnp.floor(pos[...] * (1.0 / LANES))
     hi_ref[...] = top
     lo_ref[...] = pos[...] - top * LANES
-
-    shift = (c * lrows).astype(F32)
-    lane_row = iota((1, LANES), 1).astype(F32)
-
-    def lists(i, acc):
-        left_parts, right_parts = [], []
-        for j in range(8):
-            q = pl.ds(i * 8 + j, 1)
-            at = (iota((lrows, LANES), 0).astype(F32) == hi_ref[q, :] - shift).astype(F32)
-            left_parts.append(jnp.concatenate(
-                [at * i.astype(F32), at * lane_row, at * loc_hi[q, :], at * loc_lo[q, :]], 0).astype(BF16))
-            right_parts.append(
-                (iota((LANES, LANES), 0).astype(F32) == lo_ref[q, :]).astype(F32).astype(BF16))
-        return acc + lax.dot_general(
-            jnp.concatenate(left_parts, 1), jnp.concatenate(right_parts, 1), NT, preferred_element_type=F32)
-
-    found = lax.fori_loop(0, qrows // 8, lists, jnp.zeros((4 * lrows, LANES), F32))
-    lsend[0] = (found[:lrows] * LANES + found[lrows:2 * lrows]).astype(I32)
-    lsend[1] = (found[2 * lrows:3 * lrows] * LANES + found[3 * lrows:]).astype(I32)
-    lists_at = lambda s: lbuf.at[s]
-    cross_start(lsend, lists_at, l_s, l_r)
 
     cent_wait(sq_src, sq_buf, sq_s, sq_r)
     total = sq_buf[0]
@@ -214,30 +244,30 @@
     alive = live_in[...].astype(F32)
     scale[...] = lax.rsqrt(total + 1e-6) * alive
 
-    def block_sum(b, acc):
-        weight = jnp.where(iota((blocks, LANES), 0) == b, scale[...], 0.0)
-        return acc + jnp.dot(weight, emb[pl.ds(pl.multiple_of(b * LANES, LANES), LANES), :],
-                             precision=EXACT, preferred_element_type=F32)
-
-    bsum[...] = lax.fori_loop(0, blocks, block_sum, jnp.zeros((blocks, LANES), F32))
+    weights = jnp.concatenate([scale[...], jnp.zeros((LANES - blocks, LANES), F32)], 0).T
+    for b in range(blocks):
+        bsum[b:b + 1, :] = jnp.sum(
+            weights[:, b:b + 1] * emb[b * LANES:(b + 1) * LANES, :], axis=0, keepdims=True)
     bcnt[...] = jnp.broadcast_to(jnp.sum(alive, axis=1, keepdims=True), (blocks, LANES))
     owners = [blk[b] // owned for b in range(blocks)]
     place_of = [jnp.int32(0)] + [
         jnp.where(owners[b] == owners[b - 1], 1, 0) for b in range(1, blocks)]
     local = [(blk[b] - owners[b] * owned).astype(F32) for b in range(blocks)]
 
-    def message(o, _):
-        tile = jnp.zeros((8, LANES), F32)
+    def message(i, _):
         line = iota((8, LANES), 0)
+        tiles = [jnp.zeros((8, LANES), F32)] * 4
         for b in range(blocks):
-            at = jnp.where(owners[b] == o, place_of[b], -8)
-            tile = jnp.where(line == at, bsum[b:b + 1, :], tile)
-            tile = jnp.where(line == at + 2, local[b], tile)
-            tile = jnp.where(line == at + 4, bcnt[b:b + 1, :], tile)
-        msgs[o] = tile
+            content = jnp.where(line < 2, bsum[b:b + 1, :], jnp.where(line < 4, local[b], bcnt[b:b + 1, :]))
+            for k in range(4):
+                at = jnp.where(owners[b] == i * 4 + k, place_of[b], 8)
+                mine = (line == at) | (line == at + 2) | (line == at + 4)
+                tiles[k] = jnp.where(mine, content, tiles[k])
+        for k in range(4):
+            msgs[i * 4 + k] = tiles[k]
         return 0
 
-    lax.fori_loop(0, nd, message, 0)
+    lax.fori_loop(0, nd // 4, message, 0)
 
     def a2a_start(k, _):
         to = (me + k) % nd
@@ -251,7 +281,31 @@
 
     lax.fori_loop(1, nd, a2a_start, 0)
     rbuf[me] = msgs[me]
+
+    shift = (c * lrows).astype(F32)
+    lane_row = iota((1, LANES), 1).astype(F32)
+
+    def lists(i, acc):
+        left_parts, right_parts = [], []
+        for j in range(32):
+            q = pl.ds(i * 32 + j, 1)
+            at = (iota((lrows, LANES), 0).astype(F32) == hi_ref[q, :] - shift).astype(F32)
+            left_parts.append(jnp.concatenate(
+                [at * (i * 4 + j // 8).astype(F32), at * lane_row, at * loc_hi[q, :], at * loc_lo[q, :]], 0).astype(BF16))
+            right_parts.append(
+                (iota((LANES, LANES), 0).astype(F32) == lo_ref[q, :]).astype(F32).astype(BF16))
+        return acc + lax.dot_general(
+            jnp.concatenate(left_parts, 1), jnp.concatenate(right_parts, 1), NT, preferred_element_type=F32)
+
+    found = lax.fori_loop(0, qrows // 32, lists, jnp.zeros((4 * lrows, LANES), F32))
+    lsend[0] = (found[:lrows] * LANES + found[lrows:2 * lrows]).astype(I32)
+    lsend[1] = (found[2 * lrows:3 * lrows] * LANES + found[3 * lrows:]).astype(I32)
+    lists_at = lambda s: lbuf.at[s]
+    cross_start(lsend, lists_at, l_s, l_r)
+
     forward(zr, zl, 1, 0)
+    forward(xr, xl, 1, 0)
+    forward(zr, zl, 1, 1)
     lax.fori_loop(1, nd, a2a_wait, 0)
 
     def slots(first, empty):
@@ -263,7 +317,8 @@
     slot_ids = jnp.where(slot_counts > 0, slot_ids, -1.0)
     ids_lane = slot_ids.T
     same = jnp.where((slot_ids == ids_lane) & (slot_counts > 0), 1.0, 0.0)
-    group = jnp.dot(same, sums, precision=EXACT, preferred_element_type=F32)
+    group = jnp.dot(same.astype(BF16), jnp.concatenate(split3(sums), 1), preferred_element_type=F32)
+    group = group[:, :LANES] + group[:, LANES:2 * LANES] + group[:, 2 * LANES:]
     square = group * group
     sq2_src[...] = jnp.broadcast_to(jnp.sum(square.T, axis=0, keepdims=True), (8, LANES))
     cent_start(sq2_src, sq2_buf, sq2_s, sq2_r)
@@ -272,12 +327,6 @@
         jnp.where(iota((LANES, LANES), 0) < iota((LANES, LANES), 1), same, 0.0), axis=0, keepdims=True)
     first_ids = jnp.where(earlier > 0, -1.0, ids_lane[0:1])
     counts_lane = slot_counts.T[0:1]
-    ids_top = jnp.floor(ids_lane[0:1] * (1.0 / LANES))
-    ids_low = ids_lane[0:1] - ids_top * LANES
-    count_left = jnp.where(iota(cnt.shape, 0).astype(F32) == ids_top, counts_lane, 0.0).astype(BF16)
-    count_right = (iota((LANES, LANES), 0).astype(F32) == ids_low).astype(F32).astype(BF16)
-    cnt[...] = lax.dot_general(count_left, count_right, NT, preferred_element_type=F32).astype(I32)
-
     cent_wait(sq2_src, sq2_buf, sq2_s, sq2_r)
     total2 = sq2_buf[0]
     for k in range(1, nc):
@@ -293,32 +342,29 @@
     for k in range(1, nx):
         patch_copy(k).start()
 
-    ones = jnp.ones((LANES, LANES), BF16)
-    rhs[...] = jnp.concatenate([*split3(normal), ones, *split3(group)], 1)
+    found_slots[0:SLOTS, :] = group[:SLOTS]
+    found_slots[SLOTS:2 * SLOTS, :] = normal[:SLOTS]
+    found_slots[2 * SLOTS:2 * SLOTS + 8, :] = jnp.broadcast_to(first_ids, (8, LANES))
+    found_slots[2 * SLOTS + 8:2 * SLOTS + 16, :] = jnp.broadcast_to(ids_lane[0:1], (8, LANES))
+    found_slots[2 * SLOTS + 16:2 * SLOTS + 24, :] = slot_counts.T[0:8]
+
     step = owned // 7
-
-    def picked(i, chosen, width):
-        hit = (iota((step, LANES), 0) + i * step).astype(F32) == chosen
-        return jnp.dot(hit.astype(F32).astype(BF16), rhs[:, :width], preferred_element_type=F32)
-
-    def patched(out, before):
-        new = out[:, :LANES] + out[:, LANES:2 * LANES] + out[:, 2 * LANES:3 * LANES]
-        return jnp.where(out[:, 3 * LANES:4 * LANES] > 0, new, before)
-
-    def cut(i):
-        return pl.ds(pl.multiple_of(i * step, 8), step)
-
-    def own_table(i, _):
-        out = picked(i, first_ids, 7 * LANES)
-        ms[cut(i), :] = out[:, 4 * LANES:5 * LANES] + out[:, 5 * LANES:6 * LANES] + out[:, 6 * LANES:]
-        new = patched(out, old[cut(i), :])
-        cen[cut(i), :] = new
-        own_tab[cut(i), :] = new
-        return 0
-
-    lax.fori_loop(0, 7, own_table, 0)
-    forward(xr, xl, 1, 0)
-    forward(zr, zl, 1, 1)
+    rhs[...] = rhs_of(jnp.zeros((2 * LANES, LANES), BF16))
+
+    def patch_rows(new, chosen, before, after):
+        high, low = split2(new)
+        rhs[0:SLOTS, 0:LANES] = high
+        rhs[LANES:LANES + SLOTS, 0:LANES] = low
+
+        def body(i, _):
+            at = pl.ds(pl.multiple_of(i * step, 8), step)
+            after[at, :] = replaced(chosen, rhs[...], i * step, before[at, :])
+            return 0
+
+        lax.fori_loop(0, 7, body, 0)
+
+    loads[4].wait()
+    patch_rows(normal[:SLOTS], first_ids, old, own_tab)
 
     cross_wait(lsend, lists_at, l_s, l_r)
     order = [0] + [d * s for d in range(1, nz // 2) for s in (-1, 1)] + [nz // 2]
@@ -371,14 +417,7 @@
     def patch(k, before, after):
         patch_copy(k).wait_recv()
         new = pbuf[k - 1]
-        rhs[0:SLOTS, 0:3 * LANES] = jnp.concatenate(split3(new[:SLOTS]), 1)
-        chosen = new[SLOTS:SLOTS + 1]
-
-        def body(i, _):
-            after[cut(i), :] = patched(picked(i, chosen, 4 * LANES), before[cut(i), :])
-            return 0
-
-        lax.fori_loop(0, 7, body, 0)
+        patch_rows(new[:SLOTS], new[SLOTS:SLOTS + 1], before, after)
 
     for d in (0, -1, 1):
         dots(d, 0)
@@ -406,6 +445,13 @@
         for dx in (0, -1, 1, 2):
             dots(d, dx)
         hand_on(d)
+    share = qrows // nc
+    tops = []
+    for g in range(share // 8):
+        own = [pl.ds(c * share + g * 8 + j, 1) for j in range(8)]
+        sel[:, g * 8 * LANES:(g + 1) * 8 * LANES] = jnp.concatenate(
+            [(iota((LANES, LANES), 0).astype(F32) == lo_ref[v, :]).astype(F32).astype(BF16) for v in own], 1)
+        tops.append(jnp.concatenate([hi_ref[v, :] for v in own], 1))
     zr[4, 0].wait_recv()
     zl[4, 1].wait_recv()
     for dx in (0, -1, 1, 2):
@@ -426,18 +472,12 @@
     cross_start(full, sums_at, t_s, t_r)
     cross_wait(full, sums_at, t_s, t_r)
 
-    table = jnp.concatenate(split3(tbuf[...]), 0)
-    share = qrows // nc
+    table = jnp.concatenate(split2(tbuf[...]), 0)
     for g in range(share // 8):
-        lows = [lo_ref[pl.ds(c * share + g * 8 + j, 1), :] for j in range(8)]
-        tops = [hi_ref[pl.ds(c * share + g * 8 + j, 1), :] for j in range(8)]
-        sel = jnp.concatenate(
-            [(iota((LANES, LANES), 0).astype(F32) == v).astype(F32).astype(BF16) for v in lows], 1)
-        got = jnp.dot(table, sel, preferred_element_type=F32)
-        got = got[:qrows] + got[qrows:2 * qrows] + got[2 * qrows:]
-        top_all = jnp.concatenate(tops, 1)
+        got = jnp.dot(table, sel[:, g * 8 * LANES:(g + 1) * 8 * LANES], preferred_element_type=F32)
+        got = got[:qrows] + got[qrows:]
         line = jnp.sum(
-            jnp.where(iota(got.shape, 0).astype(F32) == top_all, got, 0.0), axis=0, keepdims=True)
+            jnp.where(iota(got.shape, 0).astype(F32) == tops[g], got, 0.0), axis=0, keepdims=True)
         factor = scale[pl.ds(c * (share // 8) + g, 1), :]
         for j in range(8):
             cos[j:j + 1, g * LANES:(g + 1) * LANES] = line[:, j * LANES:(j + 1) * LANES] * factor
@@ -467,36 +507,55 @@
     dma = lambda *s: pltpu.SemaphoreType.DMA(s)
     in_vmem = pl.BlockSpec(memory_space=pltpu.VMEM)
     scratch = [
+        vmem(rows, width), vmem(owned, width), pltpu.VMEM((blocks, LANES), I32), pltpu.VMEM((cands, rows), I32),
+        pltpu.SMEM((blocks,), I32),
         [vmem(rows, width)] * (nz // 2 - 1), [vmem(rows, width)] * (nz // 2 - 1), vmem(rows, width),
         [vmem(owned, width)], [vmem(owned, width)], *[vmem(table_rows, width)] * 4,
         vmem(blocks, LANES), vmem(nc, blocks, LANES), vmem(blocks, LANES),
         vmem(blocks, LANES), vmem(blocks, LANES),
         vmem(qrows, LANES), vmem(qrows, LANES), vmem(qrows, LANES), vmem(qrows, LANES), vmem(qrows, LANES),
         vmem(nd, 8, LANES), vmem(nd, 8, LANES), vmem(8, LANES), vmem(nc, 8, LANES),
-        pltpu.VMEM((LANES, 7 * LANES), BF16), vmem(SLOTS + 8, LANES), vmem(nx - 1, SLOTS + 8, LANES),
+        pltpu.VMEM((2 * LANES, 2 * LANES), BF16), vmem(SLOTS + 8, LANES), vmem(nx - 1, SLOTS + 8, LANES),
         pltpu.VMEM((2, lrows, LANES), I32), pltpu.VMEM((nz, 2, lrows, LANES), I32),
         pltpu.SMEM((qrows, LANES), I32), pltpu.SMEM((qrows, LANES), I32),
         vmem(LANES, LANES), vmem(qrows, LANES), vmem(nc, lrows, LANES), vmem(lrows, LANES), vmem(qrows, LANES),
+        pltpu.VMEM((LANES, rows * cands // nc), BF16),
         dma(nz // 2, 2), dma(nz // 2, 2), dma(nz // 2, 2), dma(nz // 2, 2),
         dma(nx // 2, 2), dma(nx // 2, 2), dma(nx // 2, 2), dma(nx // 2, 2),
         dma(nc), dma(nc), dma(nc), dma(nc), dma(nd), dma(nd), dma(nx - 1), dma(nx - 1),
-        dma(nc), dma(nz), dma(2, nz), dma(nz), dma(nc), dma(nc), dma(nz),
+        dma(nc), dma(nz), dma(2, nz), dma(nz), dma(nc), dma(nc), dma(nz), dma(5),
     ]
-    sums, counts, cents, cosines = pl.pallas_call(
+    slots, cosines = pl.pallas_call(
         functools.partial(kernel, nd, nz, nc),
         out_shape=(
-            jax.ShapeDtypeStruct((owned, width), F32),
-            jax.ShapeDtypeStruct((-(-owned // (8 * LANES)) * 8, LANES), I32),
-            jax.ShapeDtypeStruct((owned, width), F32),
+            jax.ShapeDtypeStruct((2 * SLOTS + 24, width), F32),
             jax.ShapeDtypeStruct((cands, rows // nc), F32),
         ),
-        in_specs=[in_vmem] * 4 + [pl.BlockSpec(memory_space=pltpu.SMEM)],
-        out_specs=(in_vmem,) * 4,
+        in_specs=[pl.BlockSpec(memory_space=pltpu.HBM)] * 5,
+        out_specs=(in_vmem,) * 2,
         scratch_shapes=scratch,
         compiler_params=pltpu.CompilerParams(
-            collective_id=0, has_side_effects=True, vmem_limit_bytes=52 << 20),
+            collective_id=0, has_side_effects=True, vmem_limit_bytes=65536 * 1000),
         name="update",
     )(embeddings, old_centroids, row_mask.reshape(blocks, rows // blocks), candidates.T, block_cluster)
+    steps = 4
+    step = owned // steps
+    table_block = pl.BlockSpec((step, width), lambda i: (i, 0))
+    whole = lambda shape: pl.BlockSpec(shape, lambda i: (0, 0))
+    counts_shape = (-(-owned // (8 * LANES)) * 8, LANES)
+    sums, counts, cents = pl.pallas_call(
+        expand,
+        grid=(steps,),
+        out_shape=(
+            jax.ShapeDtypeStruct((owned, width), F32),
+            jax.ShapeDtypeStruct(counts_shape, I32),
+            jax.ShapeDtypeStruct((owned, width), F32),
+        ),
+        in_specs=[whole(slots.shape), table_block],
+        out_specs=(table_block, whole(counts_shape), table_block),
+        compiler_params=pltpu.CompilerParams(vmem_limit_bytes=16 << 20),
+        name="expand",
+    )(slots, old_centroids)
     return sums, counts.reshape(-1)[:owned], cents, cosines.T
 
 

time: 133 us -> 129 us (0.970)
  local copies, waits for them, and re-layouts: 8.56 us -> 2.9 us
  Pallas kernels: 123 us -> 125 us
    unnamed x14 -> x7, local copies, waits for them, and re-layouts: 8.56 us -> 2.9 us
    pallas_call x0 -> x1, Pallas kernels: none -> 3.06 us  [on_device(): pl.pallas_call(expand, grid=(steps,), out_shape=(jax.ShapeDtypeStruct((ow...]
    pallas_call x1, Pallas kernels: 123 us -> 122 us  [on_device(): pl.pallas_call(functools.partial(kernel, nd, nz, nc), out_shape=(jax.Shap...]
where the time goes in v2:
time: 129 us; the launch traced here: 128 us
  Pallas kernels  125 us (97%)
  local copies, waits for them, and re-layouts  2.9 us (2%)
    pallas_call x1, Pallas kernels, on_device(): pl.pallas_call(functools.partial(kernel, nd, nz, nc), out_shape=(jax.Shap...  122 us
    pallas_call x1, Pallas kernels, on_device(): pl.pallas_call(expand, grid=(steps,), out_shape=(jax.ShapeDtypeStruct((ow...  3.06 us
    unnamed x7, local copies, waits for them, and re-layouts  2.9 us

profile of v2, /device:TPU:1, one launch (start us, length us, event | category | flops | bytes accessed | tf_op | source)
XLA Modules:
  0.0 128.5 jit_solution(9899389008157316606)
XLA Ops:
  0.6 121.9 %update.1 = (f32[152,128]{1,0:T(8,128)}, f32[8,256]{1,0:T(8,128)}) custom-call(f32[2048,128]{1,0:T(8,128)} %emb_in.1, f32[3136,128]{1,0:T(8,128)} %old.1, s32[16,128]{1,0:T(8,128)} %bitcast.6, s32[8,2048]{1,0:T(8,128)} %bitcast.5, s32[16]{0:T(128)} %blk_hbm.1), custom_call_target="tpu_custom_call" | custom-call | tf_op jit(solution)/shard_map/update/pallas_call | solution.py:528
  122.5 0.0 copy-start
  122.5 1.4 %copy-done = f32[3136,128]{1,0:T(8,128)S(1)} copy-done((f32[3136,128]{1,0:T(8,128)S(1)}, f32[3136,128]{1,0:T(8,128)}, u32[]{:S(2)}) %copy-start) | copy-done | bytes 1605656
  123.9 0.0 copy-start.1
  123.9 0.9 copy-done.1
  124.8 0.0 copy-start.2
  124.8 3.1 %expand.1 = (f32[3136,128]{1,0:T(8,128)}, s32[32,128]{1,0:T(8,128)}, f32[3136,128]{1,0:T(8,128)}) custom-call(f32[152,128]{1,0:T(8,128)S(1)} %copy-done.1, f32[3136,128]{1,0:T(8,128)S(1)} %copy-done), custom_call_target="tpu_custom_call" | custom-call | tf_op jit(solution)/shard_map/expand/pallas_call | solution.py:546
  127.9 0.0 copy-done.2
  127.9 0.6 copy.10
Async XLA Ops:
  122.5 1.4 %copy-start = (f32[3136,128]{1,0:T(8,128)S(1)}, f32[3136,128]{1,0:T(8,128)}, u32[]{:S(2)}) copy-start(f32[3136,128]{1,0:T(8,128)} %old.1) | copy-start | bytes 4816900
  123.9 0.9 copy-start.1
  124.8 3.1 %copy-start.2 = (f32[8,256]{1,0:T(8,128)S(1)}, f32[8,256]{1,0:T(8,128)}, u32[]{:S(2)}) copy-start(f32[8,256]{1,0:T(8,128)} %get-tuple-element.13) | copy-start | bytes 24580

commit v3 on v2

--- a/solution.py
+++ b/solution.py
@@ -79,9 +79,9 @@
     dr, dl, dmid, tr, tl, own_tab, tmid, trp, tlp,
     sq_src, sq_buf, scale, bsum, bcnt, pos, loc_hi, loc_lo, hi_ref, lo_ref,
     msgs, rbuf, sq2_src, sq2_buf, rhs, psend, pbuf, lsend, lbuf, srow, sloc,
-    stage, part, s1buf, full, tbuf, sel,
+    stage, part, s1buf, full, tbuf, sel, obuf,
     zr_s, zr_r, zl_s, zl_r, xr_s, xr_r, xl_s, xl_r,
-    sq_s, sq_r, sq2_s, sq2_r, a2a_s, a2a_r, p_s, p_r, l_s, l_r, sm_sem, s1_s, s1_r, t_s, t_r, in_sem,
+    sq_s, sq_r, sq2_s, sq2_r, a2a_s, a2a_r, p_s, p_r, l_s, l_r, sm_sem, s1_s, s1_r, t_s, t_r, in_sem, o_s, o_r,
 ):
     nx = nd // nz
     rows, owned = emb_in.shape[0], old_in.shape[0]
@@ -113,14 +113,17 @@
     lax.fori_loop(1, nd, lambda k, _: (greet((me + k) % nd, c), 0)[1], 0)
     lax.fori_loop(1, nc, lambda k, _: (greet(me, (c + k) % nc), 0)[1], 0)
 
+    facing = (z + nz // 2) % nz
+    lax.fori_loop(1, nc, lambda k, _: (greet(x * nz + facing, (c + k) % nc), 0)[1], 0)
+
     @pl.when(c != z)
     def _():
         lax.fori_loop(1, nz, lambda k, _: (greet(x * nz + (z + k) % nz, z), 0)[1], 0)
-        pl.semaphore_wait(bar, nd - 1 + nc - 1 + nz - 1)
+        pl.semaphore_wait(bar, nd - 1 + 2 * (nc - 1) + nz - 1)
 
     @pl.when(c == z)
     def _():
-        pl.semaphore_wait(bar, nd - 1 + nc - 1)
+        pl.semaphore_wait(bar, nd - 1 + 2 * (nc - 1))
 
     def ring(n, own, right, left, mid, rs, rr, ls, lr, right_id, left_id):
         half = own.shape[0] // 2
@@ -452,25 +455,55 @@
         sel[:, g * 8 * LANES:(g + 1) * 8 * LANES] = jnp.concatenate(
             [(iota((LANES, LANES), 0).astype(F32) == lo_ref[v, :]).astype(F32).astype(BF16) for v in own], 1)
         tops.append(jnp.concatenate([hi_ref[v, :] for v in own], 1))
+    sums_at = lambda s: tbuf.at[pl.ds(pl.multiple_of(s * lrows, 8), lrows)]
+
+    @pl.when(c != facing)
+    def _():
+        def part_wait(k, _):
+            other = (c + k) % nc
+            copy(full, s1buf.at[other], s1_s.at[0], s1_r.at[other], me, other).wait_recv()
+            return 0
+
+        lax.fori_loop(1, nc, part_wait, 0)
+        total3 = s1buf[0]
+        for k in range(1, nc):
+            total3 = total3 + s1buf[k]
+        full[...] = total3
+        cross_start(full, sums_at, t_s, t_r)
+
     zr[4, 0].wait_recv()
     zl[4, 1].wait_recv()
     for dx in (0, -1, 1, 2):
         dots(4, dx)
-    hand_on(4)
-
-    def part_wait(k, _):
+    last = order.index(nz // 2)
+
+    def facing_copy(k):
         other = (c + k) % nc
-        copy(full, s1buf.at[other], s1_s.at[0], s1_r.at[other], me, other).wait_recv()
+        return copy(part.at[pl.ds(last * lrows, lrows)], obuf.at[c], o_s.at[k], o_r.at[c], x * nz + facing, other)
+
+    lax.fori_loop(0, nc, lambda k, _: (facing_copy(k).start(), 0)[1], 0)
+
+    def sums_copy(s):
+        return copy(full, sums_at(s), t_s.at[0], t_r.at[s], x * nz + c, (c + 1) % nc)
+
+    for k in range(1, nz):
+        if k != nz // 2:
+            sums_copy((z + k) % nz).wait_recv()
+
+    @pl.when(c != z)
+    def _():
+        sums_copy(z).wait_recv()
+
+    def facing_wait(k, _):
+        other = (c + k) % nc
+        copy(full, obuf.at[other], o_s.at[k], o_r.at[other], x * nz + facing, other).wait_recv()
         return 0
 
-    lax.fori_loop(1, nc, part_wait, 0)
-    total3 = s1buf[0]
+    lax.fori_loop(0, nc, facing_wait, 0)
+    total4 = obuf[0]
     for k in range(1, nc):
-        total3 = total3 + s1buf[k]
-    full[...] = total3
-    sums_at = lambda s: tbuf.at[pl.ds(pl.multiple_of(s * lrows, 8), lrows)]
-    cross_start(full, sums_at, t_s, t_r)
-    cross_wait(full, sums_at, t_s, t_r)
+        total4 = total4 + obuf[k]
+    tbuf[pl.ds(pl.multiple_of(facing * lrows, 8), lrows), :] = total4
 
     table = jnp.concatenate(split2(tbuf[...]), 0)
     for g in range(share // 8):
@@ -488,9 +521,20 @@
     for k in range(1, nx):
         patch_copy(k).wait_send()
     for i in range(nz):
-        @pl.when(source[i] != c)
-        def _(i=i):
-            part_copy(i).wait_send()
+        if i != last:
+            @pl.when(source[i] != c)
+            def _(i=i):
+                part_copy(i).wait_send()
+
+    lax.fori_loop(0, nc, lambda k, _: (facing_copy(k).wait_send(), 0)[1], 0)
+
+    @pl.when(c != facing)
+    def _():
+        lax.fori_loop(1, nc, lambda k, _: (cross_copy(full, sums_at, t_s, t_r, k).wait_send(), 0)[1], 0)
+
+        @pl.when(c != z)
+        def _():
+            cross_copy(full, sums_at, t_s, t_r, 0).wait_send()
 
 
 def on_device(nd, nc, embeddings, row_mask, block_cluster, candidates, old_centroids):
@@ -519,11 +563,11 @@
         pltpu.VMEM((2, lrows, LANES), I32), pltpu.VMEM((nz, 2, lrows, LANES), I32),
         pltpu.SMEM((qrows, LANES), I32), pltpu.SMEM((qrows, LANES), I32),
         vmem(LANES, LANES), vmem(qrows, LANES), vmem(nc, lrows, LANES), vmem(lrows, LANES), vmem(qrows, LANES),
-        pltpu.VMEM((LANES, rows * cands // nc), BF16),
+        pltpu.VMEM((LANES, rows * cands // nc), BF16), vmem(nc, lrows, LANES),
         dma(nz // 2, 2), dma(nz // 2, 2), dma(nz // 2, 2), dma(nz // 2, 2),
         dma(nx // 2, 2), dma(nx // 2, 2), dma(nx // 2, 2), dma(nx // 2, 2),
         dma(nc), dma(nc), dma(nc), dma(nc), dma(nd), dma(nd), dma(nx - 1), dma(nx - 1),
-        dma(nc), dma(nz), dma(2, nz), dma(nz), dma(nc), dma(nc), dma(nz), dma(5),
+        dma(nc), dma(nz), dma(2, nz), dma(nz), dma(nc), dma(nc), dma(nz), dma(5), dma(nc), dma(nc),
     ]
     slots, cosines = pl.pallas_call(
         functools.partial(kernel, nd, nz, nc),

time: 129 us -> 130 us (level)
    pallas_call x1, Pallas kernels: 122 us -> 123 us  [on_device(): pl.pallas_call(functools.partial(kernel, nd, nz, nc), out_shape=(jax.Shap...]
where the time goes in v3:
time: 130 us
  Pallas kernels  126 us (97%)
  local copies, waits for them, and re-layouts  2.9 us (2%)
    pallas_call x1, Pallas kernels, on_device(): pl.pallas_call(functools.partial(kernel, nd, nz, nc), out_shape=(jax.Shap...  123 us
    pallas_call x1, Pallas kernels, on_device(): pl.pallas_call(expand, grid=(steps,), out_shape=(jax.ShapeDtypeStruct((ow...  3.06 us
    unnamed x7, local copies, waits for them, and re-layouts  2.9 us

profile of v3, /device:TPU:1, one launch (start us, length us, event | category | flops | bytes accessed | tf_op | source)
XLA Modules:
  0.0 129.8 jit_solution(12774910190115813668)
XLA Ops:
  0.6 123.2 %update.1 = (f32[152,128]{1,0:T(8,128)}, f32[8,256]{1,0:T(8,128)}) custom-call(f32[2048,128]{1,0:T(8,128)} %emb_in.1, f32[3136,128]{1,0:T(8,128)} %old.1, s32[16,128]{1,0:T(8,128)} %bitcast.6, s32[8,2048]{1,0:T(8,128)} %bitcast.5, s32[16]{0:T(128)} %blk_hbm.1), custom_call_target="tpu_custom_call" | custom-call | tf_op jit(solution)/shard_map/update/pallas_call | solution.py:572
  123.9 0.0 copy-start
  123.9 1.4 %copy-done = f32[3136,128]{1,0:T(8,128)S(1)} copy-done((f32[3136,128]{1,0:T(8,128)S(1)}, f32[3136,128]{1,0:T(8,128)}, u32[]{:S(2)}) %copy-start) | copy-done | bytes 1605656
  125.3 0.0 copy-start.1
  125.3 0.9 copy-done.1
  126.2 0.0 copy-start.2
  126.2 3.1 %expand.1 = (f32[3136,128]{1,0:T(8,128)}, s32[32,128]{1,0:T(8,128)}, f32[3136,128]{1,0:T(8,128)}) custom-call(f32[152,128]{1,0:T(8,128)S(1)} %copy-done.1, f32[3136,128]{1,0:T(8,128)S(1)} %copy-done), custom_call_target="tpu_custom_call" | custom-call | tf_op jit(solution)/shard_map/expand/pallas_call | solution.py:590
  129.2 0.0 copy-done.2
  129.2 0.6 copy.10
Async XLA Ops:
  123.9 1.4 %copy-start = (f32[3136,128]{1,0:T(8,128)S(1)}, f32[3136,128]{1,0:T(8,128)}, u32[]{:S(2)}) copy-start(f32[3136,128]{1,0:T(8,128)} %old.1) | copy-start | bytes 4816900
  125.3 0.9 copy-start.1
  126.2 3.1 %copy-start.2 = (f32[8,256]{1,0:T(8,128)S(1)}, f32[8,256]{1,0:T(8,128)}, u32[]{:S(2)}) copy-start(f32[8,256]{1,0:T(8,128)} %get-tuple-element.13) | copy-start | bytes 24580
